TPU v7x, 256 devices: a whole 4x4x8 slice. The times are simulated.
256 devices in a mesh: pop: 16 (over x, z_hi, core), tp: 16 (over y, z_lo).
Axes of the slice: x: 4, y: 4, z: 8 (z_hi: 2, z_lo: 4; z = z_hi * 4 + z_lo), core: 2. Of those that a mesh axis runs over, the one named last changes fastest.
Arguments:
- left_factors: bfloat16 [16384, 4096], P(('pop', 'tp')), may hold values from -6 to 6
- right_factors: bfloat16 [16384, 16384], P('pop', 'tp'), may hold values from -6 to 6
- ranks: int32 [16384], P(('pop', 'tp')), may hold values from 0 to 16383, each once
- weight: bfloat16 [4096, 16384], P('pop', 'tp'), may hold values from -3 to 3
Outputs:
- new_weight: bfloat16 [4096, 16384], P(None, 'tp')
Inputs may be any that keep to these rules, and one draw needn't show every extreme that they name: ranks holds each of 0 to 16383 exactly once.
All inputs are finite; a program needn't handle non-finite values.
Results may differ from a plain program's by a relative error of at most 0.017.
Values may be sent and summed in bfloat16 or wider, within the bound.
A program may use at most 64 MiB of HBM per device.

v0:
```python
import math

import jax
import jax.numpy as jnp
from jax import lax
from jax.sharding import PartitionSpec as P


def outer_terms(piece, right_rows):
    return lax.dot_general(
        piece, right_rows, (((0,), (0,)), ((), ())), preferred_element_type=jnp.float32
    )


def per_device(left_factors, right_factors, ranks, weight):
    members = right_factors.shape[0]
    total = members * lax.axis_size("pop")
    score = (2.0 * ranks.astype(jnp.float32) + 1.0 - total) / total * math.sqrt(3.0 / total)
    scaled = (score[:, None] * left_factors.astype(jnp.float32)).astype(jnp.bfloat16)
    partial_value = outer_terms(lax.all_gather(scaled, "tp", axis=0, tiled=True), right_factors)
    update = lax.psum_scatter(
        partial_value.astype(jnp.bfloat16), "pop", scatter_dimension=0, tiled=True
    ).astype(jnp.float32)
    updated = (weight.astype(jnp.float32) + update).astype(jnp.bfloat16)
    return lax.all_gather(updated, "pop", axis=0, tiled=True)


def solution(mesh):
    return jax.shard_map(
        per_device,
        mesh=mesh,
        in_specs=(P(("pop", "tp"), None), P("pop", "tp"), P(("pop", "tp")), P("pop", "tp")),
        out_specs=P(None, "tp"),
        check_vma=False,
    )
```

profile of v0, /device:TPU:1, one launch (start us, length us, event | category | flops | bytes accessed | tf_op | source)
XLA Modules:
  0.0 478.3 jit_solution(13096381380432845358)
XLA Ops:
  6.5 0.0 copy-start
  6.5 0.0 all-gather.3.cloned.1.call-start
  6.5 0.8 add_multiply_fusion
  7.3 2.0 multiply_convert_fusion
  9.3 0.0 all-gather.3.cloned.1.call-update
  9.4 0.0 reduce-scatter.2.cloned.1.call-start
  9.4 191.5 %all-gather.3.cloned.1.call-done = bf16[1024,4096]{1,0:T(8,128)(2,1)} async-done(((bf16[64,4096]{1,0:T(8,128)(2,1)}), bf16[1024,4096]{1,0:T(8,128)(2,1)}) %all-gather.3.cloned.1.call-update) | async-done | bytes 8388624 | tf_op jit(solution)/shard_map/all_gather | solution.py:20
  200.9 0.0 copy-done
  200.9 14.6 %convolution_convert_fusion = bf16[4096,1024]{1,0:T(8,128)(2,1)} fusion(bf16[1024,4096]{1,0:T(8,128)(2,1)} %all-gather.3.cloned.1.call-done, bf16[1024,1024]{1,0:T(8,128)(2,1)S(1)} %copy-done), kind=kOutput, calls=%fused_computation | convolution fusion | flops 8594128896 | bytes 18874368 | tf_op jit(solution)/shard_map/dot_general | solution.py:10
  215.5 0.0 copy-start.1
  215.5 0.0 reduce-scatter.2.cloned.1.call-update
  215.5 0.0 all-gather.5.cloned.1.call-start
  215.5 140.4 %reduce-scatter.2.cloned.1.call-done = bf16[256,1024]{1,0:T(8,128)(2,1)} async-done(((bf16[4096,1024]{1,0:T(8,128)(2,1)}), bf16[256,1024]{1,0:T(8,128)(2,1)}) %reduce-scatter.2.cloned.1.call-update) | async-done | bytes 524304 | tf_op jit(solution)/shard_map/reduce_scatter | solution.py:21
  355.9 0.0 copy-done.1
  355.9 2.0 add_convert_fusion
  358.0 0.0 all-gather.5.cloned.1.call-update
  358.0 106.1 %all-gather.5.cloned.1.call-done = bf16[4096,1024]{1,0:T(8,128)(2,1)} async-done(((bf16[256,1024]{1,0:T(8,128)(2,1)}), bf16[4096,1024]{1,0:T(8,128)(2,1)}) %all-gather.5.cloned.1.call-update) | async-done | bytes 8388624 | tf_op jit(solution)/shard_map/all_gather | solution.py:25
  464.1 7.8 %copy.6 = bf16[4096,1024]{1,0:T(8,128)(2,1)} copy(bf16[4096,1024]{1,0:T(8,128)(2,1)} %all-gather.5.cloned.1.call-done) | data formatting | bytes 16777216
Async XLA Ops:
  6.5 194.4 %copy-start = (bf16[1024,1024]{1,0:T(8,128)(2,1)S(1)}, bf16[1024,1024]{1,0:T(8,128)(2,1)}, u32[]{:S(2)}) copy-start(bf16[1024,1024]{1,0:T(8,128)(2,1)} %param.5) | copy-start | bytes 6291460
  6.5 194.4 %all-gather.3.cloned.1.call-start = ((), (), s32[]{:S(2)}) async-start(), calls=%async_computation.1 | async-start | bytes 8912896 | tf_op jit(solution)/shard_map/all_gather | solution.py:20
  9.4 346.6 %reduce-scatter.2.cloned.1.call-start = ((), (), s32[]{:S(2)}) async-start(), calls=%async_computation.2 | async-start | bytes 8912896 | tf_op jit(solution)/shard_map/reduce_scatter | solution.py:21
  215.5 140.5 %copy-start.1 = (bf16[256,1024]{1,0:T(8,128)(2,1)S(1)}, bf16[256,1024]{1,0:T(8,128)(2,1)}, u32[]{:S(2)}) copy-start(bf16[256,1024]{1,0:T(8,128)(2,1)} %param.7) | copy-start | bytes 1572868
  215.5 248.6 %all-gather.5.cloned.1.call-start = ((), (), s32[]{:S(2)}) async-start(), calls=%async_computation.3 | async-start | bytes 8912896 | tf_op jit(solution)/shard_map/all_gather | solution.py:25
Sparse Core Ops, SparseCore 0:
  9.5 191.3 all-gather.2
  215.6 140.2 reduce-scatter.1
  358.6 105.3 all-gather.4
where the time goes:
time: 479 us; the launch traced here: 478 us
  waiting for transfers between devices  438 us (91%)
  matrix products  14.6 us (3%)
  between operations  13.1 us (3%)
  local copies, waits for them, and re-layouts  7.76 us (2%)
  other arithmetic  4.83 us (1%)
    all_gather x1, waiting for transfers between devices, per_device(): lax.all_gather(scaled, 'tp', axis=0, tiled=True)  191 us
    reduce_scatter x1, waiting for transfers between devices, per_device(): lax.psum_scatter(partial_value.astype(jnp.bfloat16), 'pop', scatter_dimen...  140 us
    all_gather x1, waiting for transfers between devices, per_device(): return lax.all_gather(updated, 'pop', axis=0, tiled=True)  106 us
    dot_general x1, matrix products, outer_terms(): lax.dot_general(piece, right_rows, (((0,), (0,)), ((), ())), preferred_el...  14.6 us
  transfers between devices with their start and end apart: 3, of which 3 were waited for; matrix products, arithmetic and copies ran while one was open for 0% of the time, Pallas kernels for 0%

commit v1 on v0

v1 whole, which is shorter than its diff:
```python
import functools
import math

import jax
import jax.numpy as jnp
from jax import lax
from jax.experimental import pallas as pl
from jax.experimental.pallas import tpu as pltpu
from jax.sharding import PartitionSpec as P

MESH = pl.DeviceIdType.MESH
X, ZH, CORES, Y, ZL = 4, 2, 2, 4, 4
TP = Y * ZL
CHUNKS = 8
F32, BF16 = jnp.float32, jnp.bfloat16


def kernel(
    total,
    left,
    ranks,
    right,
    weight,
    out,
    halves,
    members,
    lg,
    rall,
    wv,
    part,
    ra,
    rb,
    cl,
    cr,
    zr,
    fin,
    pre_sem,
    z_own_s,
    z_fwd_s,
    z_r,
    y1_s,
    y1_r,
    y2_s,
    y2_r,
    rs1_s,
    rs1_r,
    rs2_s,
    rs2_r,
    z4_s,
    z4_r,
    ag1_s,
    ag1_r,
    ag2_s,
    ag2_r,
    core_s,
    core_r,
    loc_s,
):
    p, t = lax.axis_index("pop"), lax.axis_index("tp")
    x, zh, c = p // 4, (p // 2) % 2, p % 2
    y, zl = t // ZL, t % ZL
    xp, xm, xo = (x + 1) % 4, (x + 3) % 4, (x + 2) % 4
    yp, ym = (y + 1) % 4, (y + 3) % 4
    J = lg.shape[0]
    DR = part.shape[3]

    def dev(x_=x, zh_=zh, c_=c, y_=y, zl_=zl):
        return (x_ * 4 + zh_ * 2 + c_, y_ * ZL + zl_)

    def rcopy(src, dst, ssem, rsem, d):
        return pltpu.make_async_remote_copy(
            src_ref=src, dst_ref=dst, send_sem=ssem, recv_sem=rsem, device_id=d, device_id_type=MESH
        )

    d_xp, d_xm, d_yp, d_ym = dev(x_=xp), dev(x_=xm), dev(y_=yp), dev(y_=ym)
    d_z4, d_c = dev(zh_=1 - zh), dev(c_=1 - c)
    d_zu, d_zd = dev(zl_=jnp.minimum(zl + 1, ZL - 1)), dev(zl_=jnp.maximum(zl - 1, 0))

    r_loc = pltpu.make_async_copy(right, rall.at[:, c], pre_sem.at[0])
    w_loc = pltpu.make_async_copy(weight, wv, pre_sem.at[1])
    r_loc.start()
    w_loc.start()

    bar = pltpu.get_barrier_semaphore()
    for d in (d_xp, d_xm, d_yp, d_ym, d_z4, d_c):
        pl.semaphore_signal(bar, 1, device_id=d, device_id_type=MESH)

    @pl.when(zl < ZL - 1)
    def _():
        pl.semaphore_signal(bar, 1, device_id=d_zu, device_id_type=MESH)

    @pl.when(zl > 0)
    def _():
        pl.semaphore_signal(bar, 1, device_id=d_zd, device_id_type=MESH)

    n_mem = left.shape[0]
    eye = lax.broadcasted_iota(jnp.int32, (n_mem, n_mem), 0) == lax.broadcasted_iota(jnp.int32, (n_mem, n_mem), 1)
    row = (2.0 * ranks[...].astype(F32) + 1.0 - total) / total * math.sqrt(3.0 / total)
    score = jnp.sum(jnp.where(eye, jnp.broadcast_to(row, (n_mem, n_mem)), 0.0), axis=1, keepdims=True)
    for m in range(8):
        for h in range(2):
            lo = 256 * (2 * m + h)
            halves[h, :, 256 * m : 256 * m + 256] = (score * left[:, lo : lo + 256].astype(F32)).astype(BF16)

    pl.semaphore_wait(bar, 6 + (zl < ZL - 1).astype(jnp.int32) + (zl > 0).astype(jnp.int32))

    m_rem = rcopy(halves.at[1 - c], members.at[c], pre_sem.at[2], pre_sem.at[3], d_c)
    m_rem.start()
    r_rem = rcopy(right, rall.at[:, c], pre_sem.at[4], pre_sem.at[5], d_c)
    r_rem.start()
    members[c] = halves[c]
    m_rem.wait_recv()

    for m in range(8):
        both = members[:, :, 256 * m : 256 * m + 256].reshape(2 * n_mem, 256)
        cols = both.astype(F32).T.astype(BF16)
        for j in range(J):
            lg[j, t, m * DR : (m + 1) * DR, :] = cols[j * DR : (j + 1) * DR]

    def z_own(j, up):
        ref = lg.at[j, t]
        return rcopy(ref, ref, z_own_s.at[j, up], z_r.at[j, zl], d_zu if up else d_zd)

    def z_fwd(j, s, up):
        ref = lg.at[j, y * ZL + s]
        return rcopy(ref, ref, z_fwd_s.at[j, s], z_r.at[j, s], d_zu if up else d_zd)

    def y1(j, s, plus):
        ref = lg.at[j, y * ZL + s]
        return rcopy(ref, ref, y1_s.at[j, plus, s], y1_r.at[j, plus, s], d_yp if plus else d_ym)

    def y1_in(j, s, plus):
        ref = lg.at[j, (ym if plus else yp) * ZL + s]
        return rcopy(ref, ref, y1_s.at[j, plus, s], y1_r.at[j, plus, s], d_yp if plus else d_ym)

    def y2(j, plus):
        b = ym * ZL if plus else yp * ZL + ZL // 2
        ref = lg.at[j, pl.ds(b, ZL // 2)]
        return rcopy(ref, ref, y2_s.at[j, plus], y2_r.at[j, plus], d_yp if plus else d_ym)

    def rs1(j, plus):
        if plus:
            return rcopy(part.at[j, xo, 0], ra.at[j], rs1_s.at[j, 1], rs1_r.at[j, 1], d_xp)
        return rcopy(part.at[j, xo, 1], rb.at[j], rs1_s.at[j, 0], rs1_r.at[j, 0], d_xm)

    def rs2(j, plus):
        if plus:
            return rcopy(part.at[j, xp], cl.at[j], rs2_s.at[j, 1], rs2_r.at[j, 1], d_xp)
        return rcopy(part.at[j, xm], cr.at[j], rs2_s.at[j, 0], rs2_r.at[j, 0], d_xm)

    def z4(j):
        return rcopy(part.at[j, x], zr.at[j], z4_s.at[j], z4_r.at[j], d_z4)

    def ag1(j, plus):
        return rcopy(fin.at[j], out.at[x, :, c, j], ag1_s.at[j, plus], ag1_r.at[j, plus], d_xp if plus else d_xm)

    def ag2(j, plus):
        ref = out.at[xm, 0, c, j] if plus else out.at[xp, 1, c, j]
        return rcopy(ref, ref, ag2_s.at[j, plus], ag2_r.at[j, plus], d_xp if plus else d_xm)

    def core(j, k):
        b = (x + k) % 4
        dst = out.at[b, :, c, j]
        return rcopy(fin.at[j] if k == 0 else dst, dst, core_s.at[j, k], core_r.at[j, k], d_c)

    def loc(j):
        return pltpu.make_async_copy(fin.at[j], out.at[x, :, c, j], loc_s.at[j])

    def st_own(j):
        @pl.when(zl < ZL - 1)
        def _():
            z_own(j, 1).start()

        @pl.when(zl > 0)
        def _():
            z_own(j, 0).start()

        y1(j, zl, 1).start()
        y1(j, zl, 0).start()

    def st_z(k, j):
        for up in (1, 0):
            s = zl - k if up else zl + k
            there = (s >= 0) if up else (s < ZL)
            on = (zl < ZL - 1) if up else (zl > 0)

            @pl.when(there)
            def _():
                z_fwd(j, s, up).wait_recv()

                @pl.when(on)
                def _():
                    z_fwd(j, s, up).start()

                y1(j, s, 1).start()
                y1(j, s, 0).start()

    def st_y2(j):
        for s in range(ZL):
            y1_in(j, s, 1).wait_recv()
        y2(j, 1).start()
        for s in range(ZL):
            y1_in(j, s, 0).wait_recv()
        y2(j, 0).start()

    def st_gemm(j):
        y2(j, 1).wait_recv()
        y2(j, 0).wait_recv()
        lhs = jnp.concatenate([lg[j, s] for s in range(TP)], axis=1)
        for n in range(4):
            rhs = rall[:, :, :, 256 * n : 256 * n + 256].reshape(TP * 2 * n_mem, 256)
            acc = jnp.dot(lhs, rhs, preferred_element_type=F32)
            part[j, :, :, :, 256 * n : 256 * n + 256] = acc.astype(BF16).reshape(X, ZH, DR, 256)
        rs1(j, 1).start()
        rs1(j, 0).start()

    def st_rs2(j):
        rs1(j, 1).wait_recv()
        part[j, xp, 0] = (part[j, xp, 0].astype(F32) + ra[j].astype(F32)).astype(BF16)
        rs2(j, 1).start()
        rs1(j, 0).wait_recv()
        part[j, xm, 1] = (part[j, xm, 1].astype(F32) + rb[j].astype(F32)).astype(BF16)
        rs2(j, 0).start()

    def st_sum(j):
        rs2(j, 1).wait_recv()
        rs2(j, 0).wait_recv()
        w = wv[j].astype(F32)
        for h in range(ZH):
            mine = part[j, x, h].astype(F32) + jnp.where(zh == h, w, 0.0)
            part[j, x, h] = (mine + cl[j, h].astype(F32) + cr[j, h].astype(F32)).astype(BF16)
        z4(j).start()

    def st_fin(j):
        z4(j).wait_recv()
        fin[j] = (part[j, x].astype(F32) + zr[j].astype(F32)).astype(BF16)
        ag1(j, 1).start()
        ag1(j, 0).start()
        core(j, 0).start()
        loc(j).start()

    def st_ag2(j):
        ag1(j, 1).wait_recv()
        ag2(j, 1).start()
        core(j, 3).start()
        ag1(j, 0).wait_recv()
        ag2(j, 0).start()
        core(j, 1).start()

    def st_last(j):
        ag2(j, 1).wait_recv()
        ag2(j, 0).wait_recv()
        core(j, 2).start()

    stages = [
        (st_last, 10),
        (st_ag2, 9),
        (st_fin, 8),
        (st_sum, 6),
        (st_rs2, 5),
        (st_gemm, 4),
        (st_y2, 3),
        (functools.partial(st_z, 3), 2),
        (functools.partial(st_z, 2), 1),
        (functools.partial(st_z, 1), 0),
    ]

    st_own(0)

    def body(i, carry):
        for fn, skew in stages:
            j = i - skew

            @pl.when(jnp.logical_and(j >= 0, j < J))
            def _():
                if fn is st_gemm:

                    @pl.when(j == 0)
                    def _():
                        r_loc.wait()
                        w_loc.wait()
                        r_rem.wait_recv()

                fn(j)

        @pl.when(i + 1 < J)
        def _():
            st_own(i + 1)

        return carry

    lax.fori_loop(0, J + 10, body, 0)

    m_rem.wait_send()
    r_rem.wait_send()

    def drain(j, carry):
        for k in range(4):
            core(j, k).wait_recv()
            core(j, k).wait_send()
        for plus in (0, 1):
            for s in range(ZL):
                y1(j, s, plus).wait_send()
            y2(j, plus).wait_send()
            rs1(j, plus).wait_send()
            rs2(j, plus).wait_send()
            ag1(j, plus).wait_send()
            ag2(j, plus).wait_send()
        z4(j).wait_send()
        loc(j).wait()

        @pl.when(zl < ZL - 1)
        def _():
            z_own(j, 1).wait_send()
            for s in range(ZL - 2):

                @pl.when(s < zl)
                def _():
                    z_fwd(j, s, 1).wait_send()

        @pl.when(zl > 0)
        def _():
            z_own(j, 0).wait_send()
            for s in range(2, ZL):

                @pl.when(s > zl)
                def _():
                    z_fwd(j, s, 0).wait_send()

        return carry

    lax.fori_loop(0, J, drain, 0)


def per_device(left_factors, right_factors, ranks, weight):
    n_mem, width = left_factors.shape
    members, cols = right_factors.shape
    total = members * lax.axis_size("pop")
    J = CHUNKS
    DR = weight.shape[0] // J
    dma = pltpu.SemaphoreType.DMA
    anyspace = pl.BlockSpec(memory_space=pl.ANY)
    vmem = pl.BlockSpec(memory_space=pltpu.VMEM)
    out = pl.pallas_call(
        functools.partial(kernel, total),
        out_shape=jax.ShapeDtypeStruct((X, ZH, CORES, J, DR, cols), BF16),
        in_specs=[vmem, vmem, anyspace, anyspace],
        out_specs=anyspace,
        scratch_shapes=[
            pltpu.VMEM((2, n_mem, width // 2), BF16),
            pltpu.VMEM((2, n_mem, width // 2), BF16),
            pltpu.VMEM((J, TP, 8 * DR, 2 * n_mem), BF16),
            pltpu.VMEM((TP, 2, n_mem, cols), BF16),
            pltpu.VMEM((J, DR, cols), BF16),
            pltpu.VMEM((J, X, ZH, DR, cols), BF16),
            pltpu.VMEM((J, DR, cols), BF16),
            pltpu.VMEM((J, DR, cols), BF16),
            pltpu.VMEM((J, ZH, DR, cols), BF16),
            pltpu.VMEM((J, ZH, DR, cols), BF16),
            pltpu.VMEM((J, ZH, DR, cols), BF16),
            pltpu.VMEM((J, ZH, DR, cols), BF16),
            dma((6,)),
            dma((J, 2)),
            dma((J, ZL)),
            dma((J, ZL)),
            dma((J, 2, ZL)),
            dma((J, 2, ZL)),
            dma((J, 2)),
            dma((J, 2)),
            dma((J, 2)),
            dma((J, 2)),
            dma((J, 2)),
            dma((J, 2)),
            dma((J,)),
            dma((J,)),
            dma((J, 2)),
            dma((J, 2)),
            dma((J, 2)),
            dma((J, 2)),
            dma((J, 4)),
            dma((J, 4)),
            dma((J,)),
        ],
        compiler_params=pltpu.CompilerParams(
            collective_id=0, has_side_effects=True, vmem_limit_bytes=48 * 2**20
        ),
    )(
        left_factors,
        ranks.reshape(1, n_mem),
        right_factors.reshape(TP, n_mem, cols),
        weight.reshape(J, DR, cols),
    )
    return out.reshape(X * ZH * CORES * J * DR, cols)


def solution(mesh):
    return jax.shard_map(
        per_device,
        mesh=mesh,
        in_specs=(P(("pop", "tp"), None), P("pop", "tp"), P(("pop", "tp")), P("pop", "tp")),
        out_specs=P(None, "tp"),
        check_vma=False,
    )
```

time: 479 us -> 145 us (0.30)
  waiting for transfers between devices: 438 us -> 0 us
  Pallas kernels: 0 us -> 133 us
  matrix products: 14.6 us -> 0 us
  between operations: 13.1 us -> 0.01 us
  other arithmetic: 4.83 us -> 0 us
    all_gather x2 -> x0, waiting for transfers between devices: 298 us -> none  [the longest x1 191 us: per_device(): lax.all_gather(scaled, 'tp', axis=0, tiled=True)]
    reduce_scatter x1 -> x0, waiting for transfers between devices: 140 us -> none  [per_device(): lax.psum_scatter(partial_value.astype(jnp.bfloat16), 'pop', scatter_dimen...]
    pallas_call x0 -> x1, Pallas kernels: none -> 133 us  [per_device(): pl.pallas_call(functools.partial(kernel, total), out_shape=jax.ShapeDtype...]
    dot_general x1 -> x0, matrix products: 14.6 us -> none  [outer_terms(): lax.dot_general(piece, right_rows, (((0,), (0,)), ((), ())), preferred_el...]
    unnamed x5 -> x9, local copies, waits for them, and re-layouts: 7.76 us -> 12.1 us
  transfers between devices with their start and end apart: 3 -> 0, of which waited for: 3 -> 0; matrix products, arithmetic and copies ran while one was open for 0% -> 0% of each run, Pallas kernels for 0% -> 0%
where the time goes in v1:
time: 145 us
  Pallas kernels  133 us (92%)
  local copies, waits for them, and re-layouts  12.1 us (8%)
    pallas_call x1, Pallas kernels, per_device(): pl.pallas_call(functools.partial(kernel, total), out_shape=jax.ShapeDtype...  133 us
    unnamed x9, local copies, waits for them, and re-layouts  12.1 us

profile of v1, /device:TPU:1, one launch (start us, length us, event | category | flops | bytes accessed | tf_op | source)
XLA Modules:
  0.0 145.0 jit_solution(12112977203081641585)
XLA Ops:
  0.0 0.0 copy-start
  0.0 1.6 %copy-done = bf16[1024,1024]{1,0:T(8,128)(2,1)S(1)} copy-done((bf16[1024,1024]{1,0:T(8,128)(2,1)S(1)}, bf16[1024,1024]{1,0:T(8,128)(2,1)}, u32[]{:S(2)}) %copy-start) | copy-done | bytes 2097176
  1.6 0.0 copy-start.1
  1.6 1.0 copy-done.1
  2.6 0.0 copy-start.2
  2.6 1.0 copy-done.2
  3.7 0.0 copy-start.3
  3.7 0.7 copy-done.3
  4.3 132.9 %shard_map.46 = bf16[4,2,2,8,32,1024]{5,4,3,2,1,0:T(8,128)(2,1)} custom-call(bf16[64,4096]{1,0:T(8,128)(2,1)S(1)} %copy-done.1, s32[1,64]{1,0:T(1,128)S(1)} %bitcast.6, bf16[16,64,1024]{2,1,0:T(8,128)(2,1)S(1)} %bitcast.4, bf16[8,32,1024]{2,1,0:T(8,128)(2,1)S(1)} %bitcast.5), custom_call_target="tpu_custom_call" | custom-call | tf_op jit(solution)/shard_map/pallas_call | solution.py:344
  137.2 7.8 %copy.6 = bf16[4096,1024]{1,0:T(8,128)(2,1)} copy(bf16[4096,1024]{1,0:T(8,128)(2,1)} %bitcast.7) | data formatting | bytes 16777216
Async XLA Ops:
  0.0 1.6 %copy-start = (bf16[1024,1024]{1,0:T(8,128)(2,1)S(1)}, bf16[1024,1024]{1,0:T(8,128)(2,1)}, u32[]{:S(2)}) copy-start(bf16[1024,1024]{1,0:T(8,128)(2,1)} %param.5) | copy-start | bytes 6291460
  1.6 1.0 copy-start.1
  2.6 1.0 copy-start.2
  3.7 0.7 copy-start.3

commit v2 on v1

v2 whole, which is shorter than its diff:
```python
import functools
import math

import jax
import jax.numpy as jnp
from jax import lax
from jax.experimental import pallas as pl
from jax.experimental.pallas import tpu as pltpu
from jax.sharding import PartitionSpec as P

MESH = pl.DeviceIdType.MESH
X, ZH, CORES, Y, ZL = 4, 2, 2, 4, 4
TP = Y * ZL
CHUNKS = 16
STEPS = 7
ORDER = (
    0x1100000, 0x2222111, 0x3333032, 0x0041404, 0x5125144, 0x3356102, 0x5712062, 0x4435763,
    0x8671600, 0x1281244, 0x9293557, 0x5608703, 0x4804356, 0x8469712, 0x9572163, 0x3782915,
    0x7362546, 0x5367948, 0x6945784, 0x6759657, 0xA867AA8, 0x7A9887A, 0x888989A, 0xAAA9999,
    0xAAAA9AA, 0xFFFFFFA,
)
F32, BF16 = jnp.float32, jnp.bfloat16


def kernel(
    total,
    left_in,
    ranks_in,
    right,
    weight,
    out,
    left,
    ranks,
    halves,
    members,
    lg,
    rall,
    wv,
    part,
    rh,
    rf,
    zr,
    pre_sem,
    z_s,
    z_r,
    y_s,
    y1_r,
    y2_r,
    rs_s,
    rs1_r,
    rs2_r,
    z4_s,
    z4_r,
    ag_s,
    ag1_r,
    ag2_r,
    core_s,
    core_r,
):
    p, t = lax.axis_index("pop"), lax.axis_index("tp")
    x, zh, c = p // 4, (p // 2) % 2, p % 2
    y, zl = t // ZL, t % ZL
    xp, xm, xo = (x + 1) % 4, (x + 3) % 4, (x + 2) % 4
    yp, ym = (y + 1) % 4, (y + 3) % 4
    J = lg.shape[0]
    DR = part.shape[3]

    def dev(x_=x, zh_=zh, c_=c, y_=y, zl_=zl):
        return (x_ * 4 + zh_ * 2 + c_, y_ * ZL + zl_)

    def rcopy(src, dst, ssem, rsem, d):
        return pltpu.make_async_remote_copy(
            src_ref=src, dst_ref=dst, send_sem=ssem, recv_sem=rsem, device_id=d, device_id_type=MESH
        )

    d_xp, d_xm, d_yp, d_ym = dev(x_=xp), dev(x_=xm), dev(y_=yp), dev(y_=ym)
    d_z4, d_c = dev(zh_=1 - zh), dev(c_=1 - c)
    d_zu, d_zd = dev(zl_=jnp.minimum(zl + 1, ZL - 1)), dev(zl_=jnp.maximum(zl - 1, 0))

    r_loc = pltpu.make_async_copy(right, rall.at[:, c], pre_sem.at[0])
    w_loc = pltpu.make_async_copy(weight, wv, pre_sem.at[1])
    left_loc = pltpu.make_async_copy(left_in, left, pre_sem.at[6])
    ranks_loc = pltpu.make_async_copy(ranks_in, ranks, pre_sem.at[7])
    ranks_loc.start()
    left_loc.start()
    r_loc.start()
    w_loc.start()

    bar = pltpu.get_barrier_semaphore()
    for d in (d_xp, d_xm, d_yp, d_ym, d_z4, d_c):
        pl.semaphore_signal(bar, 1, device_id=d, device_id_type=MESH)

    @pl.when(zl < ZL - 1)
    def _():
        pl.semaphore_signal(bar, 1, device_id=d_zu, device_id_type=MESH)

    @pl.when(zl > 0)
    def _():
        pl.semaphore_signal(bar, 1, device_id=d_zd, device_id_type=MESH)

    n_mem = left.shape[0]
    eye = lax.broadcasted_iota(jnp.int32, (n_mem, n_mem), 0) == lax.broadcasted_iota(jnp.int32, (n_mem, n_mem), 1)
    ranks_loc.wait()
    left_loc.wait()
    row = (2.0 * ranks[...].astype(F32) + 1.0 - total) / total * math.sqrt(3.0 / total)
    score = jnp.sum(jnp.where(eye, jnp.broadcast_to(row, (n_mem, n_mem)), 0.0), axis=1, keepdims=True)
    for m in range(8):
        for h in range(2):
            lo = 256 * (2 * m + h)
            halves[h, :, 256 * m : 256 * m + 256] = (score * left[:, lo : lo + 256].astype(F32)).astype(BF16)

    pl.semaphore_wait(bar, 6 + (zl < ZL - 1).astype(jnp.int32) + (zl > 0).astype(jnp.int32))

    m_rem = rcopy(halves.at[1 - c], members.at[c], pre_sem.at[2], pre_sem.at[3], d_c)
    m_rem.start()
    r_rem = rcopy(right, rall.at[:, c], pre_sem.at[4], pre_sem.at[5], d_c)
    r_rem.start()
    members[c] = halves[c]
    m_rem.wait_recv()

    for m in range(8):
        both = members[:, :, 256 * m : 256 * m + 256].reshape(2 * n_mem, 256)
        cols = both.astype(F32).T.astype(BF16)
        for j in range(J):
            lg[j, t, m * DR : (m + 1) * DR, :] = cols[j * DR : (j + 1) * DR]

    def z_own(j, up):
        ref = lg.at[j, t]
        return rcopy(ref, ref, z_s.at[j], z_r.at[j, zl], d_zu if up else d_zd)

    def z_fwd(j, s, up):
        ref = lg.at[j, y * ZL + s]
        return rcopy(ref, ref, z_s.at[j], z_r.at[j, s], d_zu if up else d_zd)

    def y1(j, s, plus):
        ref = lg.at[j, y * ZL + s]
        return rcopy(ref, ref, y_s.at[j], y1_r.at[j, plus], d_yp if plus else d_ym)

    def y1_in(j, plus):
        ref = lg.at[j, pl.ds((ym if plus else yp) * ZL, ZL)]
        return rcopy(ref, ref, y_s.at[j], y1_r.at[j, plus], d_yp if plus else d_ym)

    def y2(j, plus):
        b = ym * ZL if plus else yp * ZL + ZL // 2
        ref = lg.at[j, pl.ds(b, ZL // 2)]
        return rcopy(ref, ref, y_s.at[j], y2_r.at[j], d_yp if plus else d_ym)

    def y2_in(j):
        ref = lg.at[j, pl.ds(((y + 2) % 4) * ZL, ZL)]
        return rcopy(ref, ref, y_s.at[j], y2_r.at[j], d_yp)

    def rs1(j, plus):
        if plus:
            return rcopy(part.at[j, xo, 0], rh.at[j, 1], rs_s.at[j], rs1_r.at[j, 1], d_xp)
        return rcopy(part.at[j, xo, 1], rh.at[j, 0], rs_s.at[j], rs1_r.at[j, 0], d_xm)

    def rs2(j, plus):
        if plus:
            return rcopy(part.at[j, xp], rf.at[j, 1], rs_s.at[j], rs2_r.at[j], d_xp)
        return rcopy(part.at[j, xm], rf.at[j, 0], rs_s.at[j], rs2_r.at[j], d_xm)

    def rs2_in(j):
        return rcopy(rf.at[j], rf.at[j], rs_s.at[j], rs2_r.at[j], d_xp)

    def z4(j):
        return rcopy(part.at[j, x], zr.at[j], z4_s.at[j], z4_r.at[j], d_z4)

    def ag1(j, plus):
        ref = out.at[x, :, c, j]
        return rcopy(ref, ref, ag_s.at[j], ag1_r.at[j, plus], d_xp if plus else d_xm)

    def ag2(j, plus):
        ref = out.at[xm, 0, c, j] if plus else out.at[xp, 1, c, j]
        return rcopy(ref, ref, ag_s.at[j], ag2_r.at[j], d_xp if plus else d_xm)

    def ag2_in(j):
        ref = out.at[xo, :, c, j]
        return rcopy(ref, ref, ag_s.at[j], ag2_r.at[j], d_xp)

    def core(j, k):
        ref = out.at[(x + k) % 4, :, c, j]
        return rcopy(ref, ref, core_s.at[j], core_r.at[j], d_c)

    def drain_left(j):
        sent = lg.at[j, pl.ds(0, 3 * ZL)]
        rcopy(sent, sent, y_s.at[j], y2_r.at[j], d_yp).wait_send()
        edge = jnp.logical_or(zl == 0, zl == ZL - 1)
        for n, here in ((1, edge), (5, jnp.logical_not(edge))):

            @pl.when(here)
            def _():
                some = lg.at[j, pl.ds(0, n)]
                rcopy(some, some, z_s.at[j], z_r.at[j, 0], d_c).wait_send()

    def drain_sums(j):
        sent = part.at[j, pl.ds(0, 3)]
        rcopy(sent, sent, rs_s.at[j], rs2_r.at[j], d_xp).wait_send()

    def drain_out(j):
        sent = out.at[pl.ds(0, 3), :, c, j]
        rcopy(sent, sent, ag_s.at[j], ag2_r.at[j], d_xp).wait_send()
        z4(j).wait_send()
        sent = out.at[:, :, c, j]
        rcopy(sent, sent, core_s.at[j], core_r.at[j], d_c).wait_send()
        came = out.at[:, :, 1 - c, j]
        rcopy(came, came, core_s.at[j], core_r.at[j], d_c).wait_recv()

    def st_own(j):
        @pl.when(zl < ZL - 1)
        def _():
            z_own(j, 1).start()

        @pl.when(zl > 0)
        def _():
            z_own(j, 0).start()

        y1(j, zl, 1).start()
        y1(j, zl, 0).start()

    def st_z(k, j):
        for up in (1, 0):
            s = zl - k if up else zl + k
            there = (s >= 0) if up else (s < ZL)
            on = (zl < ZL - 1) if up else (zl > 0)

            @pl.when(there)
            def _():
                z_fwd(j, s, up).wait_recv()

                @pl.when(on)
                def _():
                    z_fwd(j, s, up).start()

                y1(j, s, 1).start()
                y1(j, s, 0).start()

    def st_y2(j):
        y1_in(j, 1).wait_recv()
        y2(j, 1).start()
        y1_in(j, 0).wait_recv()
        y2(j, 0).start()

    def st_gemm(j):
        @pl.when(j == 0)
        def _():
            r_loc.wait()
            w_loc.wait()
            r_rem.wait_recv()

        y2_in(j).wait_recv()
        lhs = jnp.concatenate([lg[j, s] for s in range(TP)], axis=1)
        for n in range(4):
            rhs = rall[:, :, :, 256 * n : 256 * n + 256].reshape(TP * 2 * n_mem, 256)
            acc = jnp.dot(lhs, rhs, preferred_element_type=F32)
            part[j, :, :, :, 256 * n : 256 * n + 256] = acc.astype(BF16).reshape(X, ZH, DR, 256)
        rs1(j, 1).start()
        rs1(j, 0).start()

    def st_rs2(j):
        rs1(j, 1).wait_recv()
        part[j, xp, 0] = (part[j, xp, 0].astype(F32) + rh[j, 1].astype(F32)).astype(BF16)
        rs2(j, 1).start()
        rs1(j, 0).wait_recv()
        part[j, xm, 1] = (part[j, xm, 1].astype(F32) + rh[j, 0].astype(F32)).astype(BF16)
        rs2(j, 0).start()

    def st_sum(j):
        rs2_in(j).wait_recv()
        w = wv[j].astype(F32)
        for h in range(ZH):
            mine = part[j, x, h].astype(F32) + jnp.where(zh == h, w, 0.0)
            part[j, x, h] = (mine + rf[j, 1, h].astype(F32) + rf[j, 0, h].astype(F32)).astype(BF16)
        z4(j).start()
        drain_left(j)

    def st_fin(j):
        z4(j).wait_recv()
        for h in range(ZH):
            out[x, h, c, j] = (part[j, x, h].astype(F32) + zr[j, h].astype(F32)).astype(BF16)
        ag1(j, 1).start()
        ag1(j, 0).start()
        core(j, 0).start()
        drain_sums(j)

    def st_ag2(j):
        ag1(j, 1).wait_recv()
        ag2(j, 1).start()
        core(j, 3).start()
        ag1(j, 0).wait_recv()
        ag2(j, 0).start()
        core(j, 1).start()

    def st_last(j):
        ag2_in(j).wait_recv()
        core(j, 2).start()

        @pl.when(j >= 2)
        def _():
            drain_out(j - 2)

    stages = (
        st_own,
        functools.partial(st_z, 1),
        functools.partial(st_z, 2),
        functools.partial(st_z, 3),
        st_y2,
        st_gemm,
        st_rs2,
        st_sum,
        st_fin,
        st_ag2,
        st_last,
    )

    def step(i, carry):
        word, counts = carry[0], carry[1:]
        now = lax.rem(word, 16)
        for n, fn in enumerate(stages):

            @pl.when(now == n)
            def _():
                fn(counts[n])

        return (lax.div(word, 16),) + tuple(
            jnp.where(now == n, count + 1, count) for n, count in enumerate(counts)
        )

    def group(g, counts):
        word = jnp.int32(ORDER[0])
        for k, w in enumerate(ORDER):
            word = jnp.where(g == k, jnp.int32(w), word)
        return lax.fori_loop(0, STEPS, step, (word,) + counts)[1:]

    lax.fori_loop(0, len(ORDER), group, (jnp.int32(0),) * len(stages))
    m_rem.wait_send()
    r_rem.wait_send()
    drain_out(J - 2)
    drain_out(J - 1)


def per_device(left_factors, right_factors, ranks, weight):
    n_mem, width = left_factors.shape
    members, cols = right_factors.shape
    total = members * lax.axis_size("pop")
    J = CHUNKS
    DR = weight.shape[0] // J
    dma = pltpu.SemaphoreType.DMA
    anyspace = pl.BlockSpec(memory_space=pl.ANY)
    vmem = pl.BlockSpec(memory_space=pltpu.VMEM)
    out = pl.pallas_call(
        functools.partial(kernel, total),
        out_shape=pltpu.VMEM((X, ZH, CORES, J, DR, cols), BF16),
        in_specs=[anyspace] * 4,
        out_specs=vmem,
        scratch_shapes=[
            pltpu.VMEM((n_mem, width), BF16),
            pltpu.VMEM((1, n_mem), jnp.int32),
            pltpu.VMEM((2, n_mem, width // 2), BF16),
            pltpu.VMEM((2, n_mem, width // 2), BF16),
            pltpu.VMEM((J, TP, 8 * DR, 2 * n_mem), BF16),
            pltpu.VMEM((TP, 2, n_mem, cols), BF16),
            pltpu.VMEM((J, DR, cols), BF16),
            pltpu.VMEM((J, X, ZH, DR, cols), BF16),
            pltpu.VMEM((J, 2, DR, cols), BF16),
            pltpu.VMEM((J, 2, ZH, DR, cols), BF16),
            pltpu.VMEM((J, ZH, DR, cols), BF16),
            dma((8,)),
            dma((J,)),
            dma((J, ZL)),
            dma((J,)),
            dma((J, 2)),
            dma((J,)),
            dma((J,)),
            dma((J, 2)),
            dma((J,)),
            dma((J,)),
            dma((J,)),
            dma((J,)),
            dma((J, 2)),
            dma((J,)),
            dma((J,)),
            dma((J,)),
        ],
        compiler_params=pltpu.CompilerParams(
            collective_id=0, has_side_effects=True, vmem_limit_bytes=48 * 2**20
        ),
    )(
        left_factors,
        ranks.reshape(1, n_mem),
        right_factors.reshape(TP, n_mem, cols),
        weight.reshape(J, DR, cols),
    )
    return out.reshape(X * ZH * CORES * J * DR, cols)


def solution(mesh):
    return jax.shard_map(
        per_device,
        mesh=mesh,
        in_specs=(P(("pop", "tp"), None), P("pop", "tp"), P(("pop", "tp")), P("pop", "tp")),
        out_specs=P(None, "tp"),
        check_vma=False,
    )
```

time: 145 us -> 121 us (0.83)
  Pallas kernels: 133 us -> 117 us
  local copies, waits for them, and re-layouts: 12.1 us -> 3.4 us
    pallas_call x1, Pallas kernels: 133 us -> 117 us  [per_device(): pl.pallas_call(functools.partial(kernel, total), out_shape=pltpu.VMEM((X,...]
    unnamed x9 -> x1, local copies, waits for them, and re-layouts: 12.1 us -> 3.4 us
where the time goes in v2:
time: 121 us; the launch traced here: 120 us
  Pallas kernels  117 us (97%)
  local copies, waits for them, and re-layouts  3.4 us (3%)
    pallas_call x1, Pallas kernels, per_device(): pl.pallas_call(functools.partial(kernel, total), out_shape=pltpu.VMEM((X,...  117 us
    unnamed x1, local copies, waits for them, and re-layouts  3.4 us

profile of v2, /device:TPU:1, one launch (start us, length us, event | category | flops | bytes accessed | tf_op | source)
XLA Modules:
  0.0 120.5 jit_solution(11880653942928944567)
XLA Ops:
  0.0 117.1 %shard_map.46 = bf16[4,2,2,16,16,1024]{5,4,3,2,1,0:T(8,128)(2,1)S(1)} custom-call(bf16[64,4096]{1,0:T(8,128)(2,1)} %left_in.1, s32[1,64]{1,0:T(1,128)} %bitcast.7, bf16[16,64,1024]{2,1,0:T(8,128)(2,1)} %bitcast.5, bf16[16,16,1024]{2,1,0:T(8,128)(2,1)} %bitcast.6), custom_call_target="tpu_custom_call" | custom-call | tf_op jit(solution)/shard_map/pallas_call | solution.py:350
  117.1 3.4 %copy.6 = bf16[4096,1024]{1,0:T(8,128)(2,1)} copy(bf16[4096,1024]{1,0:T(8,128)(2,1)S(1)} %bitcast.4) | data formatting | bytes 16777216

commit v3 on v2

--- a/solution.py
+++ b/solution.py
@@ -14,10 +14,10 @@
 CHUNKS = 16
 STEPS = 7
 ORDER = (
-    0x1100000, 0x2222111, 0x3333032, 0x0041404, 0x5125144, 0x3356102, 0x5712062, 0x4435763,
-    0x8671600, 0x1281244, 0x9293557, 0x5608703, 0x4804356, 0x8469712, 0x9572163, 0x3782915,
-    0x7362546, 0x5367948, 0x6945784, 0x6759657, 0xA867AA8, 0x7A9887A, 0x888989A, 0xAAA9999,
-    0xAAAA9AA, 0xFFFFFFA,
+    0x1110110, 0x2111100, 0x1211102, 0x0230033, 0x0450454, 0x3062025, 0x3254603, 0x0726224,
+    0x4672350, 0x3427853, 0x5436283, 0x2568497, 0x5608379, 0x2837944, 0x538756A, 0x87B99A6,
+    0x624A546, 0x4A7589B, 0x63BA357, 0xB679181, 0x958944A, 0xA75876B, 0x97896C1, 0xB7CCA68,
+    0xA8B9789, 0x9ABAC89, 0xCCABB9A, 0xBCAABAC, 0xBBCCBCB, 0xFFCCCCC,
 )
 F32, BF16 = jnp.float32, jnp.bfloat16
 
@@ -29,9 +29,7 @@
     right,
     weight,
     out,
-    left,
     ranks,
-    halves,
     members,
     lg,
     rall,
@@ -79,10 +77,14 @@
 
     r_loc = pltpu.make_async_copy(right, rall.at[:, c], pre_sem.at[0])
     w_loc = pltpu.make_async_copy(weight, wv, pre_sem.at[1])
-    left_loc = pltpu.make_async_copy(left_in, left, pre_sem.at[6])
-    ranks_loc = pltpu.make_async_copy(ranks_in, ranks, pre_sem.at[7])
+    ranks_loc = pltpu.make_async_copy(ranks_in, ranks.at[c], pre_sem.at[2])
     ranks_loc.start()
-    left_loc.start()
+
+    def left_block(m, half):
+        return left_in.at[:, pl.ds(pl.multiple_of(256 * (2 * m + half), 256), 256)]
+
+    for m in range(8):
+        pltpu.make_async_copy(left_block(m, c), members.at[c, :, pl.ds(256 * m, 256)], pre_sem.at[3]).start()
     r_loc.start()
     w_loc.start()
 
@@ -98,29 +100,31 @@
     def _():
         pl.semaphore_signal(bar, 1, device_id=d_zd, device_id_type=MESH)
 
-    n_mem = left.shape[0]
-    eye = lax.broadcasted_iota(jnp.int32, (n_mem, n_mem), 0) == lax.broadcasted_iota(jnp.int32, (n_mem, n_mem), 1)
-    ranks_loc.wait()
-    left_loc.wait()
-    row = (2.0 * ranks[...].astype(F32) + 1.0 - total) / total * math.sqrt(3.0 / total)
-    score = jnp.sum(jnp.where(eye, jnp.broadcast_to(row, (n_mem, n_mem)), 0.0), axis=1, keepdims=True)
+    pl.semaphore_wait(bar, 6 + (zl < ZL - 1).astype(jnp.int32) + (zl > 0).astype(jnp.int32))
+
+    ranks_rem = rcopy(ranks_in, ranks.at[c], pre_sem.at[6], pre_sem.at[7], d_c)
+    ranks_rem.start()
     for m in range(8):
-        for h in range(2):
-            lo = 256 * (2 * m + h)
-            halves[h, :, 256 * m : 256 * m + 256] = (score * left[:, lo : lo + 256].astype(F32)).astype(BF16)
-
-    pl.semaphore_wait(bar, 6 + (zl < ZL - 1).astype(jnp.int32) + (zl > 0).astype(jnp.int32))
-
-    m_rem = rcopy(halves.at[1 - c], members.at[c], pre_sem.at[2], pre_sem.at[3], d_c)
-    m_rem.start()
+        rcopy(left_block(m, 1 - c), members.at[c, :, pl.ds(256 * m, 256)], pre_sem.at[8], pre_sem.at[9], d_c).start()
     r_rem = rcopy(right, rall.at[:, c], pre_sem.at[4], pre_sem.at[5], d_c)
     r_rem.start()
-    members[c] = halves[c]
+
+    n_mem = left_in.shape[0]
+    m_rem = rcopy(members.at[c], members.at[c], pre_sem.at[8], pre_sem.at[9], d_c)
+    ranks_loc.wait()
+    ranks_rem.wait_recv()
+    eye = lax.broadcasted_iota(jnp.int32, (n_mem, n_mem), 0) == lax.broadcasted_iota(jnp.int32, (n_mem, n_mem), 1)
+    scores = []
+    for k in range(CORES):
+        row = (2.0 * ranks[k].astype(F32) + 1.0 - total) / total * math.sqrt(3.0 / total)
+        row = jnp.where(eye, jnp.broadcast_to(row, (n_mem, n_mem)), 0.0)
+        scores.append(jnp.sum(row, axis=1, keepdims=True))
+    score = jnp.concatenate(scores, axis=0)
+    pltpu.make_async_copy(members.at[c], members.at[c], pre_sem.at[3]).wait()
     m_rem.wait_recv()
-
     for m in range(8):
-        both = members[:, :, 256 * m : 256 * m + 256].reshape(2 * n_mem, 256)
-        cols = both.astype(F32).T.astype(BF16)
+        both = members[:, :, 256 * m : 256 * m + 256].reshape(2 * n_mem, 256).astype(F32)
+        cols = (score * both).astype(BF16).astype(F32).T.astype(BF16)
         for j in range(J):
             lg[j, t, m * DR : (m + 1) * DR, :] = cols[j * DR : (j + 1) * DR]
 
@@ -205,7 +209,7 @@
         came = out.at[:, :, 1 - c, j]
         rcopy(came, came, core_s.at[j], core_r.at[j], d_c).wait_recv()
 
-    def st_own(j):
+    def st_own_z(j):
         @pl.when(zl < ZL - 1)
         def _():
             z_own(j, 1).start()
@@ -214,6 +218,7 @@
         def _():
             z_own(j, 0).start()
 
+    def st_own_y(j):
         y1(j, zl, 1).start()
         y1(j, zl, 0).start()
 
@@ -231,8 +236,11 @@
                 def _():
                     z_fwd(j, s, up).start()
 
-                y1(j, s, 1).start()
-                y1(j, s, 0).start()
+    def st_y1(j):
+        for k in range(1, ZL):
+            s = (zl + k) % ZL
+            y1(j, s, 1).start()
+            y1(j, s, 0).start()
 
     def st_y2(j):
         y1_in(j, 1).wait_recv()
@@ -299,10 +307,12 @@
             drain_out(j - 2)
 
     stages = (
-        st_own,
+        st_own_z,
+        st_own_y,
         functools.partial(st_z, 1),
         functools.partial(st_z, 2),
         functools.partial(st_z, 3),
+        st_y1,
         st_y2,
         st_gemm,
         st_rs2,
@@ -333,6 +343,7 @@
 
     lax.fori_loop(0, len(ORDER), group, (jnp.int32(0),) * len(stages))
     m_rem.wait_send()
+    ranks_rem.wait_send()
     r_rem.wait_send()
     drain_out(J - 2)
     drain_out(J - 1)
@@ -353,9 +364,7 @@
         in_specs=[anyspace] * 4,
         out_specs=vmem,
         scratch_shapes=[
-            pltpu.VMEM((n_mem, width), BF16),
-            pltpu.VMEM((1, n_mem), jnp.int32),
-            pltpu.VMEM((2, n_mem, width // 2), BF16),
+            pltpu.VMEM((2, 1, n_mem), jnp.int32),
             pltpu.VMEM((2, n_mem, width // 2), BF16),
             pltpu.VMEM((J, TP, 8 * DR, 2 * n_mem), BF16),
             pltpu.VMEM((TP, 2, n_mem, cols), BF16),
@@ -364,7 +373,7 @@
             pltpu.VMEM((J, 2, DR, cols), BF16),
             pltpu.VMEM((J, 2, ZH, DR, cols), BF16),
             pltpu.VMEM((J, ZH, DR, cols), BF16),
-            dma((8,)),
+            dma((10,)),
             dma((J,)),
             dma((J, ZL)),
             dma((J,)),

time: 121 us -> 117 us (0.967)
  Pallas kernels: 117 us -> 113 us
    pallas_call x1, Pallas kernels: 117 us -> 113 us  [per_device(): pl.pallas_call(functools.partial(kernel, total), out_shape=pltpu.VMEM((X,...]
where the time goes in v3:
time: 117 us
  Pallas kernels  113 us (97%)
  local copies, waits for them, and re-layouts  3.4 us (3%)
    pallas_call x1, Pallas kernels, per_device(): pl.pallas_call(functools.partial(kernel, total), out_shape=pltpu.VMEM((X,...  113 us
    unnamed x1, local copies, waits for them, and re-layouts  3.4 us

profile of v3, /device:TPU:1, one launch (start us, length us, event | category | flops | bytes accessed | tf_op | source)
XLA Modules:
  0.0 116.9 jit_solution(4516597383493655381)
XLA Ops:
  0.0 113.4 %shard_map.46 = bf16[4,2,2,16,16,1024]{5,4,3,2,1,0:T(8,128)(2,1)S(1)} custom-call(bf16[64,4096]{1,0:T(8,128)(2,1)} %left_in.1, s32[1,64]{1,0:T(1,128)} %bitcast.7, bf16[16,64,1024]{2,1,0:T(8,128)(2,1)} %bitcast.5, bf16[16,16,1024]{2,1,0:T(8,128)(2,1)} %bitcast.6), custom_call_target="tpu_custom_call" | custom-call | tf_op jit(solution)/shard_map/pallas_call | solution.py:361
  113.5 3.4 %copy.6 = bf16[4096,1024]{1,0:T(8,128)(2,1)} copy(bf16[4096,1024]{1,0:T(8,128)(2,1)S(1)} %bitcast.4) | data formatting | bytes 16777216

commit v4 on v3

--- a/solution.py
+++ b/solution.py
@@ -14,11 +14,12 @@
 CHUNKS = 16
 STEPS = 7
 ORDER = (
-    0x1110110, 0x2111100, 0x1211102, 0x0230033, 0x0450454, 0x3062025, 0x3254603, 0x0726224,
-    0x4672350, 0x3427853, 0x5436283, 0x2568497, 0x5608379, 0x2837944, 0x538756A, 0x87B99A6,
-    0x624A546, 0x4A7589B, 0x63BA357, 0xB679181, 0x958944A, 0xA75876B, 0x97896C1, 0xB7CCA68,
-    0xA8B9789, 0x9ABAC89, 0xCCABB9A, 0xBCAABAC, 0xBBCCBCB, 0xFFCCCCC,
+    0x0110110, 0x1111010, 0x5403210, 0x5410302, 0x2256432, 0x5126430, 0x2203720, 0x2054736,
+    0x4226383, 0x9607538, 0x6897354, 0x4873254, 0x0A56320, 0xA564897, 0xB368794, 0x689B475,
+    0x6875A32, 0x82754A9, 0x6CB9113, 0x68375A4, 0x7C54BA9, 0xCA56481, 0x9AC8179, 0x6BB8796,
+    0x79B879B, 0xAA89CA8, 0xC9CAB9A, 0xAACCBAB, 0xBBBCCBB, 0xFFCCCCC,
 )
+DIRECT = 4
 F32, BF16 = jnp.float32, jnp.bfloat16
 
 
@@ -92,15 +93,10 @@
     for d in (d_xp, d_xm, d_yp, d_ym, d_z4, d_c):
         pl.semaphore_signal(bar, 1, device_id=d, device_id_type=MESH)
 
-    @pl.when(zl < ZL - 1)
-    def _():
-        pl.semaphore_signal(bar, 1, device_id=d_zu, device_id_type=MESH)
-
-    @pl.when(zl > 0)
-    def _():
-        pl.semaphore_signal(bar, 1, device_id=d_zd, device_id_type=MESH)
-
-    pl.semaphore_wait(bar, 6 + (zl < ZL - 1).astype(jnp.int32) + (zl > 0).astype(jnp.int32))
+    for k in range(1, ZL):
+        pl.semaphore_signal(bar, 1, device_id=dev(zl_=(zl + k) % ZL), device_id_type=MESH)
+
+    pl.semaphore_wait(bar, 6 + ZL - 1)
 
     ranks_rem = rcopy(ranks_in, ranks.at[c], pre_sem.at[6], pre_sem.at[7], d_c)
     ranks_rem.start()
@@ -132,6 +128,10 @@
         ref = lg.at[j, t]
         return rcopy(ref, ref, z_s.at[j], z_r.at[j, zl], d_zu if up else d_zd)
 
+    def z_direct(j, q):
+        ref = lg.at[j, t]
+        return rcopy(ref, ref, z_s.at[j], z_r.at[j, zl], dev(zl_=q))
+
     def z_fwd(j, s, up):
         ref = lg.at[j, y * ZL + s]
         return rcopy(ref, ref, z_s.at[j], z_r.at[j, s], d_zu if up else d_zd)
@@ -188,8 +188,10 @@
     def drain_left(j):
         sent = lg.at[j, pl.ds(0, 3 * ZL)]
         rcopy(sent, sent, y_s.at[j], y2_r.at[j], d_yp).wait_send()
+        line = j >= DIRECT
         edge = jnp.logical_or(zl == 0, zl == ZL - 1)
-        for n, here in ((1, edge), (5, jnp.logical_not(edge))):
+        inner = jnp.logical_not(edge)
+        for n, here in ((3, j < DIRECT), (1, jnp.logical_and(line, edge)), (5, jnp.logical_and(line, inner))):
 
             @pl.when(here)
             def _():
@@ -210,13 +212,15 @@
         rcopy(came, came, core_s.at[j], core_r.at[j], d_c).wait_recv()
 
     def st_own_z(j):
-        @pl.when(zl < ZL - 1)
+        @pl.when(j < DIRECT)
         def _():
-            z_own(j, 1).start()
-
-        @pl.when(zl > 0)
+            for q in range(ZL):
+                pl.when(zl != q)(lambda: z_direct(j, q).start())
+
+        @pl.when(j >= DIRECT)
         def _():
-            z_own(j, 0).start()
+            pl.when(zl < ZL - 1)(lambda: z_own(j, 1).start())
+            pl.when(zl > 0)(lambda: z_own(j, 0).start())
 
     def st_own_y(j):
         y1(j, zl, 1).start()
@@ -226,7 +230,7 @@
         for up in (1, 0):
             s = zl - k if up else zl + k
             there = (s >= 0) if up else (s < ZL)
-            on = (zl < ZL - 1) if up else (zl > 0)
+            on = jnp.logical_and(j >= DIRECT, (zl < ZL - 1) if up else (zl > 0))
 
             @pl.when(there)
             def _():

time: 117 us -> 116 us (level)
  no operation moved by 1% of the time
where the time goes in v4:
time: 116 us
  Pallas kernels  112 us (97%)
  local copies, waits for them, and re-layouts  3.4 us (3%)
    pallas_call x1, Pallas kernels, per_device(): pl.pallas_call(functools.partial(kernel, total), out_shape=pltpu.VMEM((X,...  112 us
    unnamed x1, local copies, waits for them, and re-layouts  3.4 us

profile of v4, /device:TPU:1, one launch (start us, length us, event | category | flops | bytes accessed | tf_op | source)
XLA Modules:
  0.0 115.7 jit_solution(7158713826548186166)
XLA Ops:
  0.0 112.3 %shard_map.46 = bf16[4,2,2,16,16,1024]{5,4,3,2,1,0:T(8,128)(2,1)S(1)} custom-call(bf16[64,4096]{1,0:T(8,128)(2,1)} %left_in.1, s32[1,64]{1,0:T(1,128)} %bitcast.7, bf16[16,64,1024]{2,1,0:T(8,128)(2,1)} %bitcast.5, bf16[16,16,1024]{2,1,0:T(8,128)(2,1)} %bitcast.6), custom_call_target="tpu_custom_call" | custom-call | tf_op jit(solution)/shard_map/pallas_call | solution.py:365
  112.3 3.4 %copy.6 = bf16[4096,1024]{1,0:T(8,128)(2,1)} copy(bf16[4096,1024]{1,0:T(8,128)(2,1)S(1)} %bitcast.4) | data formatting | bytes 16777216

commit v5 on v4

--- a/solution.py
+++ b/solution.py
@@ -14,10 +14,10 @@
 CHUNKS = 16
 STEPS = 7
 ORDER = (
-    0x0110110, 0x1111010, 0x5403210, 0x5410302, 0x2256432, 0x5126430, 0x2203720, 0x2054736,
-    0x4226383, 0x9607538, 0x6897354, 0x4873254, 0x0A56320, 0xA564897, 0xB368794, 0x689B475,
-    0x6875A32, 0x82754A9, 0x6CB9113, 0x68375A4, 0x7C54BA9, 0xCA56481, 0x9AC8179, 0x6BB8796,
-    0x79B879B, 0xAA89CA8, 0xC9CAB9A, 0xAACCBAB, 0xBBBCCBB, 0xFFCCCCC,
+    0x0111110, 0x3210011, 0x3201054, 0x0600541, 0x6325432, 0x7520042, 0x0023162, 0x2654387,
+    0x5437203, 0x8562498, 0x2436973, 0x469A875, 0xA234875, 0x87B3956, 0xA1B5469, 0x5426087,
+    0x608793A, 0x51C4BA3, 0x1867B92, 0x8352A74, 0xA171B69, 0x6854B93, 0xBC58497, 0x6879A6C,
+    0x79B879A, 0xBA989A8, 0xACACB9A, 0xCCBACAB, 0xCBBBCCB, 0xFFCCCCC,
 )
 DIRECT = 4
 F32, BF16 = jnp.float32, jnp.bfloat16
@@ -185,6 +185,10 @@
         ref = out.at[(x + k) % 4, :, c, j]
         return rcopy(ref, ref, core_s.at[j], core_r.at[j], d_c)
 
+    def core_all(j):
+        ref = out.at[:, :, c, j]
+        return rcopy(ref, ref, core_s.at[j], core_r.at[j], d_c)
+
     def drain_left(j):
         sent = lg.at[j, pl.ds(0, 3 * ZL)]
         rcopy(sent, sent, y_s.at[j], y2_r.at[j], d_yp).wait_send()
@@ -291,24 +295,25 @@
             out[x, h, c, j] = (part[j, x, h].astype(F32) + zr[j, h].astype(F32)).astype(BF16)
         ag1(j, 1).start()
         ag1(j, 0).start()
-        core(j, 0).start()
+        pl.when(j >= J - 2)(lambda: core(j, 0).start())
         drain_sums(j)
 
     def st_ag2(j):
         ag1(j, 1).wait_recv()
         ag2(j, 1).start()
-        core(j, 3).start()
         ag1(j, 0).wait_recv()
         ag2(j, 0).start()
-        core(j, 1).start()
+
+        @pl.when(j >= J - 2)
+        def _():
+            core(j, 3).start()
+            core(j, 1).start()
 
     def st_last(j):
         ag2_in(j).wait_recv()
-        core(j, 2).start()
-
-        @pl.when(j >= 2)
-        def _():
-            drain_out(j - 2)
+        pl.when(j >= J - 2)(lambda: core(j, 2).start())
+        pl.when(j < J - 2)(lambda: core_all(j).start())
+        pl.when(j >= 2)(lambda: drain_out(j - 2))
 
     stages = (
         st_own_z,

time: 116 us -> 115 us (level)
  no operation moved by 1% of the time
where the time goes in v5:
time: 115 us
  Pallas kernels  111 us (97%)
  local copies, waits for them, and re-layouts  3.4 us (3%)
    pallas_call x1, Pallas kernels, per_device(): pl.pallas_call(functools.partial(kernel, total), out_shape=pltpu.VMEM((X,...  111 us
    unnamed x1, local copies, waits for them, and re-layouts  3.4 us

profile of v5, /device:TPU:1, one launch (start us, length us, event | category | flops | bytes accessed | tf_op | source)
XLA Modules:
  0.0 114.7 jit_solution(16326009207183284491)
XLA Ops:
  0.0 111.3 %shard_map.46 = bf16[4,2,2,16,16,1024]{5,4,3,2,1,0:T(8,128)(2,1)S(1)} custom-call(bf16[64,4096]{1,0:T(8,128)(2,1)} %left_in.1, s32[1,64]{1,0:T(1,128)} %bitcast.7, bf16[16,64,1024]{2,1,0:T(8,128)(2,1)} %bitcast.5, bf16[16,16,1024]{2,1,0:T(8,128)(2,1)} %bitcast.6), custom_call_target="tpu_custom_call" | custom-call | tf_op jit(solution)/shard_map/pallas_call | solution.py:370
  111.3 3.4 %copy.6 = bf16[4096,1024]{1,0:T(8,128)(2,1)} copy(bf16[4096,1024]{1,0:T(8,128)(2,1)S(1)} %bitcast.4) | data formatting | bytes 16777216

commit v6 on v5

--- a/solution.py
+++ b/solution.py
@@ -14,12 +14,12 @@
 CHUNKS = 16
 STEPS = 7
 ORDER = (
-    0x0111110, 0x3210011, 0x3201054, 0x0600541, 0x6325432, 0x7520042, 0x0023162, 0x2654387,
-    0x5437203, 0x8562498, 0x2436973, 0x469A875, 0xA234875, 0x87B3956, 0xA1B5469, 0x5426087,
-    0x608793A, 0x51C4BA3, 0x1867B92, 0x8352A74, 0xA171B69, 0x6854B93, 0xBC58497, 0x6879A6C,
-    0x79B879A, 0xBA989A8, 0xACACB9A, 0xCCBACAB, 0xCBBBCCB, 0xFFCCCCC,
+    0x1111101, 0x0101010, 0x0015432, 0x1252432, 0x2132060, 0x5402630, 0x5473203, 0x5406227,
+    0x3823348, 0x6497506, 0x2834795, 0x8725036, 0x72596A4, 0x52968A4, 0xB87B433, 0x73A9605,
+    0x3514986, 0xB78546A, 0x6AB9472, 0x8317485, 0x91B796A, 0x817A568, 0xC67B549, 0x79869A8,
+    0x8C7C9BA, 0xCCB89AC, 0x9AAAB9C, 0xBAABBAC, 0xBBBCCCB, 0xFFCCCCC,
 )
-DIRECT = 4
+DIRECT = 2
 F32, BF16 = jnp.float32, jnp.bfloat16
 
 
@@ -76,25 +76,21 @@
     d_z4, d_c = dev(zh_=1 - zh), dev(c_=1 - c)
     d_zu, d_zd = dev(zl_=jnp.minimum(zl + 1, ZL - 1)), dev(zl_=jnp.maximum(zl - 1, 0))
 
-    r_loc = pltpu.make_async_copy(right, rall.at[:, c], pre_sem.at[0])
-    w_loc = pltpu.make_async_copy(weight, wv, pre_sem.at[1])
-    ranks_loc = pltpu.make_async_copy(ranks_in, ranks.at[c], pre_sem.at[2])
-    ranks_loc.start()
-
-    def left_block(m, half):
-        return left_in.at[:, pl.ds(pl.multiple_of(256 * (2 * m + half), 256), 256)]
-
-    for m in range(8):
-        pltpu.make_async_copy(left_block(m, c), members.at[c, :, pl.ds(256 * m, 256)], pre_sem.at[3]).start()
-    r_loc.start()
-    w_loc.start()
-
     bar = pltpu.get_barrier_semaphore()
     for d in (d_xp, d_xm, d_yp, d_ym, d_z4, d_c):
         pl.semaphore_signal(bar, 1, device_id=d, device_id_type=MESH)
 
     for k in range(1, ZL):
         pl.semaphore_signal(bar, 1, device_id=dev(zl_=(zl + k) % ZL), device_id_type=MESH)
+
+    ranks_loc = pltpu.make_async_copy(ranks_in, ranks.at[c], pre_sem.at[2])
+    ranks_loc.start()
+
+    def left_block(m, half):
+        return left_in.at[:, pl.ds(pl.multiple_of(256 * (2 * m + half), 256), 256)]
+
+    for m in range(8):
+        pltpu.make_async_copy(left_block(m, c), members.at[c, :, pl.ds(256 * m, 256)], pre_sem.at[3]).start()
 
     pl.semaphore_wait(bar, 6 + ZL - 1)
 
@@ -103,7 +99,11 @@
     for m in range(8):
         rcopy(left_block(m, 1 - c), members.at[c, :, pl.ds(256 * m, 256)], pre_sem.at[8], pre_sem.at[9], d_c).start()
     r_rem = rcopy(right, rall.at[:, c], pre_sem.at[4], pre_sem.at[5], d_c)
+    r_loc = pltpu.make_async_copy(right, rall.at[:, c], pre_sem.at[0])
+    w_loc = pltpu.make_async_copy(weight, wv, pre_sem.at[1])
     r_rem.start()
+    r_loc.start()
+    w_loc.start()
 
     n_mem = left_in.shape[0]
     m_rem = rcopy(members.at[c], members.at[c], pre_sem.at[8], pre_sem.at[9], d_c)

time: 115 us -> 115 us (level)
  no operation moved by 1% of the time
where the time goes in v6:
time: 115 us
  Pallas kernels  112 us (97%)
  local copies, waits for them, and re-layouts  3.4 us (3%)
    pallas_call x1, Pallas kernels, per_device(): pl.pallas_call(functools.partial(kernel, total), out_shape=pltpu.VMEM((X,...  112 us
    unnamed x1, local copies, waits for them, and re-layouts  3.4 us

profile of v6, /device:TPU:1, one launch (start us, length us, event | category | flops | bytes accessed | tf_op | source)
XLA Modules:
  0.0 114.9 jit_solution(1142191207055458728)
XLA Ops:
  0.0 111.5 %shard_map.46 = bf16[4,2,2,16,16,1024]{5,4,3,2,1,0:T(8,128)(2,1)S(1)} custom-call(bf16[64,4096]{1,0:T(8,128)(2,1)} %left_in.1, s32[1,64]{1,0:T(1,128)} %bitcast.7, bf16[16,64,1024]{2,1,0:T(8,128)(2,1)} %bitcast.5, bf16[16,16,1024]{2,1,0:T(8,128)(2,1)} %bitcast.6), custom_call_target="tpu_custom_call" | custom-call | tf_op jit(solution)/shard_map/pallas_call | solution.py:370
  111.5 3.4 %copy.6 = bf16[4096,1024]{1,0:T(8,128)(2,1)} copy(bf16[4096,1024]{1,0:T(8,128)(2,1)S(1)} %bitcast.4) | data formatting | bytes 16777216

commit v7 on v6

--- a/solution.py
+++ b/solution.py
@@ -310,6 +310,12 @@
             core(j, 1).start()
 
     def st_last(j):
+        @pl.when(j == 0)
+        def _():
+            m_rem.wait_send()
+            ranks_rem.wait_send()
+            r_rem.wait_send()
+
         ag2_in(j).wait_recv()
         pl.when(j >= J - 2)(lambda: core(j, 2).start())
         pl.when(j < J - 2)(lambda: core_all(j).start())
@@ -351,9 +357,6 @@
         return lax.fori_loop(0, STEPS, step, (word,) + counts)[1:]
 
     lax.fori_loop(0, len(ORDER), group, (jnp.int32(0),) * len(stages))
-    m_rem.wait_send()
-    ranks_rem.wait_send()
-    r_rem.wait_send()
     drain_out(J - 2)
     drain_out(J - 1)
 

time: 115 us -> 115 us (level)
  no operation moved by 1% of the time
where the time goes in v7:
time: 115 us
  Pallas kernels  112 us (97%)
  local copies, waits for them, and re-layouts  3.4 us (3%)
    pallas_call x1, Pallas kernels, per_device(): pl.pallas_call(functools.partial(kernel, total), out_shape=pltpu.VMEM((X,...  112 us
    unnamed x1, local copies, waits for them, and re-layouts  3.4 us

profile of v7, /device:TPU:1, one launch (start us, length us, event | category | flops | bytes accessed | tf_op | source)
XLA Modules:
  0.0 115.0 jit_solution(14325000300771590086)
XLA Ops:
  0.0 111.5 %shard_map.46 = bf16[4,2,2,16,16,1024]{5,4,3,2,1,0:T(8,128)(2,1)S(1)} custom-call(bf16[64,4096]{1,0:T(8,128)(2,1)} %left_in.1, s32[1,64]{1,0:T(1,128)} %bitcast.7, bf16[16,64,1024]{2,1,0:T(8,128)(2,1)} %bitcast.5, bf16[16,16,1024]{2,1,0:T(8,128)(2,1)} %bitcast.6), custom_call_target="tpu_custom_call" | custom-call | tf_op jit(solution)/shard_map/pallas_call | solution.py:373
  111.6 3.4 %copy.6 = bf16[4096,1024]{1,0:T(8,128)(2,1)} copy(bf16[4096,1024]{1,0:T(8,128)(2,1)S(1)} %bitcast.4) | data formatting | bytes 16777216
